TPU v7x, 32 devices: a whole 2x2x4 slice. The times are simulated.
32 devices in a mesh: uly: 4 (over y, x), blk: 8 (over z, core).
Axes of the slice: x: 2, y: 2, z: 4, core: 2. Of those that a mesh axis runs over, the one named last changes fastest.
Arguments:
- query_rows: bfloat16 [12288, 512], P(('uly', 'blk')), may hold values from -8 to 8
- key_rows: bfloat16 [12288, 512], P(('uly', 'blk')), may hold values from -8 to 8
- value_rows: bfloat16 [12288, 512], P(('uly', 'blk')), may hold values from -6 to 6
- kept_tiles: int32 [32, 6], replicated, may hold values from -1 to 31, as said below
Outputs:
- attended: bfloat16 [12288, 512], P(('uly', 'blk'))
Inputs may be any that keep to these rules, and one draw needn't show every extreme that they name: `kept_tiles`: tile t = p * 8 + a with p = b * 4 + c has coordinates (b, a, c) with 0 <= b < 1, 0 <= a < 8, 0 <= c < 4; slab a is the tiles with that a, and p is a tile's position in its slab. Row t lists distinct tiles, t itself first, then the others, then -1 in the unused entries; every listed tile differs from t by at most 1 in each coordinate. For every slab a and each of the slabs a - 1 and a + 1, the tiles of that neighbouring slab listed by queries of slab a lie within 2 consecutive positions. Some row fills all 6 entries.
All inputs are finite; a program needn't handle non-finite values.
Results may differ from a plain program's by a relative error of at most 0.0047.
Values may be sent and summed in bfloat16 or wider, within the bound.
A program may use at most 64 MiB of HBM per device.

v0:
```python
import jax
import jax.numpy as jnp
from jax import lax
from jax.sharding import PartitionSpec as P

HEAD_DIM = 128
TILE = 384
KEEP = 6


def passed_along(block, axis, distance):
    devices = range(lax.axis_size(axis))
    route = [(i - distance, i) for i in devices if i - distance in devices]
    return lax.ppermute(block, axis, route)


def tile_place(tile_ids, n_blk):
    slab_of = tile_ids % n_blk
    position = tile_ids // n_blk
    return (slab_of, position)


def slab_kept(kept_tiles, slab_index, n_blk, slab_tiles):
    position = jnp.arange(slab_tiles, dtype=jnp.int32)
    tile_ids = position * n_blk + slab_index
    return jnp.take(kept_tiles, tile_ids, axis=0)


def body(query_rows, key_rows, value_rows, kept_tiles):
    query_local, key_local, value_local = (
        lax.all_to_all(query_rows, "uly", split_axis=1, concat_axis=0, tiled=True),
        lax.all_to_all(key_rows, "uly", split_axis=1, concat_axis=0, tiled=True),
        lax.all_to_all(value_rows, "uly", split_axis=1, concat_axis=0, tiled=True),
    )
    n_uly = lax.axis_size("uly")
    n_blk = lax.axis_size("blk")
    feat_width = query_local.shape[1]
    head_dev = feat_width // HEAD_DIM
    slab_now = lax.axis_index("blk")
    score_scale = HEAD_DIM ** (-0.5)
    listed = slab_kept(kept_tiles, slab_now, n_blk, n_uly)
    is_live = listed >= 0
    slab_of, position = tile_place(jnp.where(is_live, listed, 0), n_blk)
    relative = slab_of - slab_now
    key_tiles = key_local.reshape(n_uly, TILE, feat_width)
    value_tiles = value_local.reshape(n_uly, TILE, feat_width)
    left_key, left_value = passed_along((key_tiles, value_tiles), "blk", 1)
    right_key, right_value = passed_along((key_tiles, value_tiles), "blk", -1)
    key_buffer = jnp.concatenate([left_key, key_tiles, right_key], axis=0)
    value_buffer = jnp.concatenate([left_value, value_tiles, right_value], axis=0)
    buffer_slot = (relative + 1) * n_uly + position
    buffer_slot = jnp.where(is_live, buffer_slot, 0)
    key_buffer = key_buffer.reshape(-1, TILE, head_dev, HEAD_DIM)
    value_buffer = value_buffer.reshape(-1, TILE, head_dev, HEAD_DIM)
    tile_group = 1
    while tile_group * TILE < 512 and n_uly % (tile_group * 2) == 0:
        tile_group = tile_group * 2
    block_count = n_uly // tile_group
    query_blocks = query_local.reshape(block_count, tile_group, TILE, head_dev, HEAD_DIM)
    slot_blocks = buffer_slot.reshape(block_count, tile_group, KEEP)
    live_blocks = is_live.reshape(block_count, tile_group, KEEP)

    def attend_block(block_args):
        query_block, slot_block, live_block = block_args
        key_gather = key_buffer[slot_block].reshape(tile_group, KEEP * TILE, head_dev, HEAD_DIM)
        value_gather = value_buffer[slot_block].reshape(tile_group, KEEP * TILE, head_dev, HEAD_DIM)
        scores = (
            jnp.einsum(
                "gihd,gjhd->ghij", query_block, key_gather, preferred_element_type=jnp.float32
            )
            * score_scale
        )
        live_cols = jnp.repeat(live_block, TILE, axis=1)
        scores = jnp.where(live_cols[:, None, None, :], scores, -jnp.inf)
        row_max = jnp.max(scores, axis=3, keepdims=True)
        weights = jnp.exp(scores - row_max)
        totals = jnp.sum(weights, axis=3)
        weights_low = weights.astype(jnp.bfloat16)
        mixed = jnp.einsum(
            "ghij,gjhd->gihd", weights_low, value_gather, preferred_element_type=jnp.float32
        )
        mixed = mixed / jnp.transpose(totals, (0, 2, 1))[:, :, :, None]
        return mixed.astype(jnp.bfloat16)

    attended = lax.map(attend_block, (query_blocks, slot_blocks, live_blocks))
    attended = attended.reshape(n_uly * TILE, feat_width)
    return lax.all_to_all(attended, "uly", split_axis=0, concat_axis=1, tiled=True)


def solution(mesh):
    placed = (P(("uly", "blk"), None), P(("uly", "blk"), None), P(("uly", "blk"), None), P())
    return jax.shard_map(
        body, mesh=mesh, in_specs=placed, out_specs=P(("uly", "blk"), None), check_vma=False
    )
```

profile of v0, /device:TPU:1, one launch (start us, length us, event | category | flops | bytes accessed | tf_op | source)
XLA Modules:
  0.0 81.1 jit_solution(17358343100803055592)
XLA Ops:
  0.0 2.0 %copy.30 = bf16[384,512]{0,1:T(8,128)(2,1)} copy(bf16[384,512]{1,0:T(8,128)(2,1)} %param.7) | data formatting | bytes 786432 | tf_op args[1]
  2.0 4.4 %all-to-all-start.2 = ((bf16[384,4,128]{0,2,1:T(8,128)(2,1)}), bf16[384,4,128]{0,2,1:T(8,128)(2,1)S(1)}, u32[]{:S(2)}, u32[]{:S(2)}) async-start(bf16[384,4,128]{0,2,1:T(8,128)(2,1)} %bitcast.17), calls=%async_computation.2 | async-start | bytes 786432 | tf_op jit(solution)/shard_map/all_to_all | solution.py:32
  6.4 0.9 %copy.27 = bf16[384,512]{0,1:T(8,128)(2,1)} copy(bf16[384,512]{1,0:T(8,128)(2,1)S(1)} %copy-done.3) | data formatting | bytes 786432 | tf_op args[2]
  7.3 4.8 %all-to-all-done.2 = bf16[384,4,128]{0,2,1:T(8,128)(2,1)S(1)} async-done(((bf16[384,4,128]{0,2,1:T(8,128)(2,1)}), bf16[384,4,128]{0,2,1:T(8,128)(2,1)S(1)}, u32[]{:S(2)}, u32[]{:S(2)}) %all-to-all-start.2) | async-done | bytes 393248 | tf_op jit(solution)/shard_map/all_to_all | solution.py:32
  12.1 3.5 %all-to-all-start = ((bf16[384,4,128]{0,2,1:T(8,128)(2,1)}), bf16[384,4,128]{0,2,1:T(8,128)(2,1)S(1)}, u32[]{:S(2)}, u32[]{:S(2)}) async-start(bf16[384,4,128]{0,2,1:T(8,128)(2,1)} %bitcast.12), calls=%async_computation | async-start | bytes 786432 | tf_op jit(solution)/shard_map/all_to_all | solution.py:33
  16.3 0.8 %copy_bitcast_fusion = bf16[384,4,128]{2,0,1:T(8,128)(2,1)} fusion(bf16[384,512]{1,0:T(8,128)(2,1)S(1)} %copy-done), kind=kLoop, calls=%fused_computation.27 | loop fusion | bytes 786432 | tf_op jit(solution)/shard_map/all_to_all | solution.py:31
  17.1 4.9 %collective-permute-start.2 = (bf16[4,384,128]{1,2,0:T(8,128)(2,1)S(1)}, bf16[4,384,128]{1,2,0:T(8,128)(2,1)S(1)}, u32[]{:S(2)}, u32[]{:S(2)}) collective-permute-start(bf16[4,384,128]{1,2,0:T(8,128)(2,1)S(1)} %bitcast.89), channel_id=1, source_target_pairs={{0,1},{1,2},{2,3},{3,4},{4,5},{5,6},{6,7},{8,9},{9,10},{10,11},{11... | collective-permute-start | bytes 1179656 | tf_op jit(solution)/shard_map/ppermute | solution.py:14
  22.0 1.9 %collective-permute-start.3 = (bf16[4,384,128]{1,2,0:T(8,128)(2,1)S(1)}, bf16[4,384,128]{1,2,0:T(8,128)(2,1)S(1)}, u32[]{:S(2)}, u32[]{:S(2)}) collective-permute-start(bf16[4,384,128]{1,2,0:T(8,128)(2,1)S(1)} %bitcast.90), channel_id=1, source_target_pairs={{1,0},{2,1},{3,2},{4,3},{5,4},{6,5},{7,6},{9,8},{10,9},{11,10},{12... | collective-permute-start | bytes 1179656 | tf_op jit(solution)/shard_map/ppermute | solution.py:14
  23.9 3.9 %all-to-all-start.1 = ((bf16[384,4,128]{2,0,1:T(8,128)(2,1)}), bf16[384,4,128]{2,0,1:T(8,128)(2,1)S(1)}, u32[]{:S(2)}, u32[]{:S(2)}) async-start(bf16[384,4,128]{2,0,1:T(8,128)(2,1)} %copy_bitcast_fusion), calls=%async_computation.1 | async-start | bytes 786432 | tf_op jit(solution)/shard_map/all_to_all | solution.py:31
  27.8 3.9 %collective-permute-start = (bf16[4,384,128]{1,2,0:T(8,128)(2,1)S(1)}, bf16[4,384,128]{1,2,0:T(8,128)(2,1)}, u32[]{:S(2)}, u32[]{:S(2)}) collective-permute-start(bf16[4,384,128]{1,2,0:T(8,128)(2,1)S(1)} %bitcast.92), channel_id=1, source_target_pairs={{0,1},{1,2},{2,3},{3,4},{4,5},{5,6},{6,7},{8,9},{9,10},{10,11},{11... | collective-permute-start | bytes 1179656 | tf_op jit(solution)/shard_map/ppermute | solution.py:14
  31.8 1.9 %collective-permute-start.1 = (bf16[4,384,128]{1,2,0:T(8,128)(2,1)S(1)}, bf16[4,384,128]{1,2,0:T(8,128)(2,1)}, u32[]{:S(2)}, u32[]{:S(2)}) collective-permute-start(bf16[4,384,128]{1,2,0:T(8,128)(2,1)S(1)} %bitcast.93), channel_id=1, source_target_pairs={{1,0},{2,1},{3,2},{4,3},{5,4},{6,5},{7,6},{9,8},{10,9},{11,10},{12... | collective-permute-start | bytes 1179656 | tf_op jit(solution)/shard_map/ppermute | solution.py:14
  33.8 0.6 fusion.27
  34.6 0.8 copy.31
  35.3 1.1 %collective-permute-done = bf16[4,384,128]{1,2,0:T(8,128)(2,1)} collective-permute-done((bf16[4,384,128]{1,2,0:T(8,128)(2,1)S(1)}, bf16[4,384,128]{1,2,0:T(8,128)(2,1)}, u32[]{:S(2)}, u32[]{:S(2)}) %collective-permute-start) | collective-permute-done | bytes 393248 | tf_op jit(solution)/shard_map/ppermute | solution.py:14
  36.5 4.5 %collective-permute-done.1 = bf16[4,384,128]{1,2,0:T(8,128)(2,1)} collective-permute-done((bf16[4,384,128]{1,2,0:T(8,128)(2,1)S(1)}, bf16[4,384,128]{1,2,0:T(8,128)(2,1)}, u32[]{:S(2)}, u32[]{:S(2)}) %collective-permute-start.1) | collective-permute-done | bytes 393248 | tf_op jit(solution)/shard_map/ppermute | solution.py:14
  41.0 1.3 %pad_maximum_fusion = bf16[12,384,128]{1,2,0:T(8,128)(2,1)S(1)} fusion(bf16[4,384,128]{1,2,0:T(8,128)(2,1)} %collective-permute-done.1, bf16[4,384,128]{1,2,0:T(8,128)(2,1)S(1)} %bitcast.94, bf16[4,384,128]{1,2,0:T(8,128)(2,1)} %collective-permute-done), kind=kLoop, calls=%fused_computation.25 | loop fusion | flops 1179648 | bytes 2359296 | tf_op jit(solution)/shard_map/concatenate | solution.py:50
  42.2 1.5 %copy.28 = bf16[12,384,128]{2,1,0:T(8,128)(2,1)} copy(bf16[12,384,128]{1,2,0:T(8,128)(2,1)S(1)} %pad_maximum_fusion) | data formatting | bytes 2359296 | tf_op jit(solution)/shard_map/concatenate | solution.py:50
  43.7 27.2 %while.10 = (s32[]{:T(128)}, bf16[2,2,384,1,128]{4,2,1,0,3:T(8,128)(2,1)S(1)}, s32[2,2,6]{2,1,0:T(2,128)S(1)}, bf16[12,384,1,128]{3,1,0,2:T(8,128)(2,1)}, pred[2...) while((s32[]{:T(128)}, ...), condition=%wide.region_3.4_spmd, body=%wide.region_0.3_spmd.sunk | while | flops 925629952 | bytes 62590820 | solution.py:85
  44.3 0.8 gather_fusion.1
  45.1 0.6 dynamic-slice_bitcast_fusion.2
  45.8 1.2 %fusion.41 = (f32[2,384]{1,0:T(2,128)S(1)}, f32[2,384,2304]{2,1,0:T(8,128)S(1)}) fusion(pred[2,2304]{1,0:T(4,128)(4,1)S(1)} %bitcast.86, bf16[2,2304,128]{2,1,0:T(8,128)(2,1)S(1)} %bitcast.79, bf16[2,2,384,1,128]{4,2,1,3,0:T(8,128)(2,1)S(1)} %get-tuple-element.127, s32[]{:T(128)} %get-tuple-element.114), kind=kOutput, calls=%fused_computation.5.clone.1 | convolution fusion | flops 458292480 | bytes 8466436 | tf_op jit(solution)/shard_map/while/body/eval_jaxpr/gihd,gjhd->ghij/dot_general | solution.py:68
  47.1 2.8 %fusion.42 = f32[2,384]{1,0:T(2,128)} fusion(f32[2,384,2304]{2,1,0:T(8,128)S(1)} %get-tuple-element.104, f32[2,384]{1,0:T(2,128)S(1)} %get-tuple-element.105, pred[2,2304]{1,0:T(4,128)(4,1)S(1)} %bitcast.87), kind=kLoop, calls=%fused_computation.6.clone.1 | loop fusion | flops 7077120 | bytes 7088640 | tf_op jit(solution)/shard_map/while/body/eval_jaxpr/reduce_sum | solution.py:77
  49.9 2.0 %gather_fusion = bf16[12,384,128]{2,1,0:T(8,128)(2,1)} fusion(bf16[12,384,128]{2,1,0:T(8,128)(2,1)S(1)} %bitcast.83, s32[1024]{0:T(1024)} %copy-done.5), kind=kCustom, calls=%fused_computation.clone.1 | custom fusion | bytes 2359344 | tf_op jit(solution)/shard_map/while/body/eval_jaxpr/gather | solution.py:66
  51.9 5.2 %fusion.43 = bf16[1,2,384,1,128]{2,4,1,3,0:T(8,128)(2,1)S(1)} fusion(bf16[2,2304,128]{2,1,0:T(8,128)(2,1)} %bitcast.84, f32[2,384,2304]{2,1,0:T(8,128)} %copy-done.1, f32[2,384]{1,0:T(2,128)S(1)} %get-tuple-element.105, pred[2,2304]{1,0:T(4,128)(4,1)S(1)} %bitcast.88, f32[2,384]{1,0:T(2,128)} %fusion.42), kind=kOutput, calls=%fused_computation.13.clone.1 | convolution fusion | flops 460259328 | bytes 8464896 | tf_op jit(solution)/shard_map/while/body/eval_jaxpr/ghij,gjhd->gihd/dot_general | solution.py:79
  57.9 0.8 gather_fusion.1
  58.7 0.6 dynamic-slice_bitcast_fusion.2
  59.4 1.2 %fusion.41 = (f32[2,384]{1,0:T(2,128)S(1)}, f32[2,384,2304]{2,1,0:T(8,128)S(1)}) fusion(pred[2,2304]{1,0:T(4,128)(4,1)S(1)} %bitcast.86, bf16[2,2304,128]{2,1,0:T(8,128)(2,1)S(1)} %bitcast.79, bf16[2,2,384,1,128]{4,2,1,3,0:T(8,128)(2,1)S(1)} %get-tuple-element.127, s32[]{:T(128)} %get-tuple-element.114), kind=kOutput, calls=%fused_computation.5.clone.1 | convolution fusion | flops 458292480 | bytes 8466436 | tf_op jit(solution)/shard_map/while/body/eval_jaxpr/gihd,gjhd->ghij/dot_general | solution.py:68
  60.7 2.8 %fusion.42 = f32[2,384]{1,0:T(2,128)} fusion(f32[2,384,2304]{2,1,0:T(8,128)S(1)} %get-tuple-element.104, f32[2,384]{1,0:T(2,128)S(1)} %get-tuple-element.105, pred[2,2304]{1,0:T(4,128)(4,1)S(1)} %bitcast.87), kind=kLoop, calls=%fused_computation.6.clone.1 | loop fusion | flops 7077120 | bytes 7088640 | tf_op jit(solution)/shard_map/while/body/eval_jaxpr/reduce_sum | solution.py:77
  63.6 2.0 %gather_fusion = bf16[12,384,128]{2,1,0:T(8,128)(2,1)} fusion(bf16[12,384,128]{2,1,0:T(8,128)(2,1)S(1)} %bitcast.83, s32[1024]{0:T(1024)} %copy-done.5), kind=kCustom, calls=%fused_computation.clone.1 | custom fusion | bytes 2359344 | tf_op jit(solution)/shard_map/while/body/eval_jaxpr/gather | solution.py:66
  65.5 5.2 %fusion.43 = bf16[1,2,384,1,128]{2,4,1,3,0:T(8,128)(2,1)S(1)} fusion(bf16[2,2304,128]{2,1,0:T(8,128)(2,1)} %bitcast.84, f32[2,384,2304]{2,1,0:T(8,128)} %copy-done.1, f32[2,384]{1,0:T(2,128)S(1)} %get-tuple-element.105, pred[2,2304]{1,0:T(4,128)(4,1)S(1)} %bitcast.88, f32[2,384]{1,0:T(2,128)} %fusion.42), kind=kOutput, calls=%fused_computation.13.clone.1 | convolution fusion | flops 460259328 | bytes 8464896 | tf_op jit(solution)/shard_map/while/body/eval_jaxpr/ghij,gjhd->gihd/dot_general | solution.py:79
  71.0 9.0 %all_to_all.67 = bf16[4,384,128]{2,1,0:T(8,128)(2,1)S(1)} all-to-all(bf16[4,384,128]{2,1,0:T(8,128)(2,1)S(1)} %bitcast.96), channel_id=1, replica_groups=mesh['uly'=4,'blk'=8] {'uly'}, dimensions={0} | all-to-all | bytes 786432 | tf_op jit(solution)/shard_map/all_to_all | solution.py:87
  80.2 0.9 %copy.34 = bf16[384,512]{1,0:T(8,128)(2,1)} copy(bf16[384,512]{0,1:T(8,128)(2,1)S(1)} %bitcast.95) | data formatting | bytes 786432 | tf_op jit(solution)/shard_map/all_to_all | solution.py:87
  (55 shorter events, 3.1 us)
Async XLA Ops:
  0.0 16.3 %copy-start = (bf16[384,512]{1,0:T(8,128)(2,1)S(1)}, bf16[384,512]{1,0:T(8,128)(2,1)}, u32[]{:S(2)}) copy-start(bf16[384,512]{1,0:T(8,128)(2,1)} %param.6) | copy-start | bytes 1179652
  0.0 6.4 %copy-start.3 = (bf16[384,512]{1,0:T(8,128)(2,1)S(1)}, bf16[384,512]{1,0:T(8,128)(2,1)}, u32[]{:S(2)}) copy-start(bf16[384,512]{1,0:T(8,128)(2,1)} %param.8) | copy-start | bytes 1179652
  2.0 13.6 %copy-start.8 = (s32[32,6]{0,1:T(8,128)S(1)}, s32[32,6]{0,1:T(8,128)}, u32[]{:S(2)}) copy-start(s32[32,6]{0,1:T(8,128)} %param.9) | copy-start | bytes 2308
  2.0 10.1 %all-to-all-start.2 = ((bf16[384,4,128]{0,2,1:T(8,128)(2,1)}), bf16[384,4,128]{0,2,1:T(8,128)(2,1)S(1)}, u32[]{:S(2)}, u32[]{:S(2)}) async-start(bf16[384,4,128]{0,2,1:T(8,128)(2,1)} %bitcast.17), calls=%async_computation.2 | async-start | bytes 786432 | tf_op jit(solution)/shard_map/all_to_all | solution.py:32
  12.1 11.8 %all-to-all-start = ((bf16[384,4,128]{0,2,1:T(8,128)(2,1)}), bf16[384,4,128]{0,2,1:T(8,128)(2,1)S(1)}, u32[]{:S(2)}, u32[]{:S(2)}) async-start(bf16[384,4,128]{0,2,1:T(8,128)(2,1)} %bitcast.12), calls=%async_computation | async-start | bytes 786432 | tf_op jit(solution)/shard_map/all_to_all | solution.py:33
  17.1 17.3 %collective-permute-start.2 = (bf16[4,384,128]{1,2,0:T(8,128)(2,1)S(1)}, bf16[4,384,128]{1,2,0:T(8,128)(2,1)S(1)}, u32[]{:S(2)}, u32[]{:S(2)}) collective-permute-start(bf16[4,384,128]{1,2,0:T(8,128)(2,1)S(1)} %bitcast.89), channel_id=1, source_target_pairs={{0,1},{1,2},{2,3},{3,4},{4,5},{5,6},{6,7},{8,9},{9,10},{10,11},{11... | collective-permute-start | bytes 1179656 | tf_op jit(solution)/shard_map/ppermute | solution.py:14
  22.0 12.4 %collective-permute-start.3 = (bf16[4,384,128]{1,2,0:T(8,128)(2,1)S(1)}, bf16[4,384,128]{1,2,0:T(8,128)(2,1)S(1)}, u32[]{:S(2)}, u32[]{:S(2)}) collective-permute-start(bf16[4,384,128]{1,2,0:T(8,128)(2,1)S(1)} %bitcast.90), channel_id=1, source_target_pairs={{1,0},{2,1},{3,2},{4,3},{5,4},{6,5},{7,6},{9,8},{10,9},{11,10},{12... | collective-permute-start | bytes 1179656 | tf_op jit(solution)/shard_map/ppermute | solution.py:14
  23.9 19.8 %all-to-all-start.1 = ((bf16[384,4,128]{2,0,1:T(8,128)(2,1)}), bf16[384,4,128]{2,0,1:T(8,128)(2,1)S(1)}, u32[]{:S(2)}, u32[]{:S(2)}) async-start(bf16[384,4,128]{2,0,1:T(8,128)(2,1)} %copy_bitcast_fusion), calls=%async_computation.1 | async-start | bytes 786432 | tf_op jit(solution)/shard_map/all_to_all | solution.py:31
  27.8 8.6 %collective-permute-start = (bf16[4,384,128]{1,2,0:T(8,128)(2,1)S(1)}, bf16[4,384,128]{1,2,0:T(8,128)(2,1)}, u32[]{:S(2)}, u32[]{:S(2)}) collective-permute-start(bf16[4,384,128]{1,2,0:T(8,128)(2,1)S(1)} %bitcast.92), channel_id=1, source_target_pairs={{0,1},{1,2},{2,3},{3,4},{4,5},{5,6},{6,7},{8,9},{9,10},{10,11},{11... | collective-permute-start | bytes 1179656 | tf_op jit(solution)/shard_map/ppermute | solution.py:14
  31.8 9.2 %collective-permute-start.1 = (bf16[4,384,128]{1,2,0:T(8,128)(2,1)S(1)}, bf16[4,384,128]{1,2,0:T(8,128)(2,1)}, u32[]{:S(2)}, u32[]{:S(2)}) collective-permute-start(bf16[4,384,128]{1,2,0:T(8,128)(2,1)S(1)} %bitcast.93), channel_id=1, source_target_pairs={{1,0},{2,1},{3,2},{4,3},{5,4},{6,5},{7,6},{9,8},{10,9},{11,10},{12... | collective-permute-start | bytes 1179656 | tf_op jit(solution)/shard_map/ppermute | solution.py:14
  42.2 1.5 %copy-start.4 = (bf16[2,2,384,1,128]{4,2,1,0,3:T(8,128)(2,1)S(1)}, bf16[2,2,384,1,128]{4,2,1,0,3:T(8,128)(2,1)}, u32[]{:S(2)}) copy-start(bf16[2,2,384,1,128]{4,2,1,0,3:T(8,128)(2,1)} %custom-call.6) | copy-start | bytes 1179652
  43.7 0.6 copy-start.6
  43.9 1.3 %copy-start.5 = (s32[1024]{0:T(1024)}, s32[1024]{0:T(1024)S(1)}, u32[]{:S(2)}) copy-start(s32[1024]{0:T(1024)S(1)} %pad_clamp_fusion.3) | copy-start | bytes 12292 | tf_op jit(solution)/shard_map/while
  47.0 2.9 %copy-start.1 = (f32[2,384,2304]{2,1,0:T(8,128)}, f32[2,384,2304]{2,1,0:T(8,128)S(1)}, u32[]{:S(2)}) copy-start(f32[2,384,2304]{2,1,0:T(8,128)S(1)} %get-tuple-element.104) | copy-start | bytes 21233668 | tf_op jit(solution)/shard_map/while
  47.1 2.9 %copy-start.2 = (bf16[12,384,1,128]{3,1,0,2:T(8,128)(2,1)S(1)}, bf16[12,384,1,128]{3,1,0,2:T(8,128)(2,1)}, u32[]{:S(2)}) copy-start(bf16[12,384,1,128]{3,1,0,2:T(8,128)(2,1)} %get-tuple-element.125) | copy-start | bytes 3538948 | tf_op jit(solution)/shard_map/while
  51.9 5.4 %copy-start.7 = (s32[2,2,6]{2,1,0:T(2,128)S(1)}, s32[2,2,6]{2,1,0:T(2,128)}, u32[]{:S(2)}) copy-start(s32[2,2,6]{2,1,0:T(2,128)} %copy-done.6) | copy-start | bytes 292 | tf_op jit(solution)/shard_map/while
  57.3 0.6 copy-start.6
  57.4 1.3 %copy-start.5 = (s32[1024]{0:T(1024)}, s32[1024]{0:T(1024)S(1)}, u32[]{:S(2)}) copy-start(s32[1024]{0:T(1024)S(1)} %pad_clamp_fusion.3) | copy-start | bytes 12292 | tf_op jit(solution)/shard_map/while
  60.7 2.9 %copy-start.1 = (f32[2,384,2304]{2,1,0:T(8,128)}, f32[2,384,2304]{2,1,0:T(8,128)S(1)}, u32[]{:S(2)}) copy-start(f32[2,384,2304]{2,1,0:T(8,128)S(1)} %get-tuple-element.104) | copy-start | bytes 21233668 | tf_op jit(solution)/shard_map/while
  60.7 2.9 %copy-start.2 = (bf16[12,384,1,128]{3,1,0,2:T(8,128)(2,1)S(1)}, bf16[12,384,1,128]{3,1,0,2:T(8,128)(2,1)}, u32[]{:S(2)}) copy-start(bf16[12,384,1,128]{3,1,0,2:T(8,128)(2,1)} %get-tuple-element.125) | copy-start | bytes 3538948 | tf_op jit(solution)/shard_map/while
  65.5 5.4 %copy-start.7 = (s32[2,2,6]{2,1,0:T(2,128)S(1)}, s32[2,2,6]{2,1,0:T(2,128)}, u32[]{:S(2)}) copy-start(s32[2,2,6]{2,1,0:T(2,128)} %copy-done.6) | copy-start | bytes 292 | tf_op jit(solution)/shard_map/while
where the time goes:
time: 82.2 us; the launch traced here: 81.1 us
  starting transfers between devices  24.4 us (30%)
  local copies, waits for them, and re-layouts  16.4 us (20%)
  matrix products  12.8 us (16%)
  waiting for transfers between devices  10.4 us (13%)
  blocking collectives  8.99 us (11%)
  other arithmetic  7.78 us (9%)
    ppermute x4, starting transfers between devices, passed_along(): return lax.ppermute(block, axis, route)  12.7 us
    dot_general x2, matrix products, attend_block(): jnp.einsum('ghij,gjhd->gihd', weights_low, value_gather, preferred_elemen...  10.4 us
    all_to_all x1, blocking collectives, body(): lax.all_to_all(attended, 'uly', split_axis=0, concat_axis=1, tiled=True)  8.99 us
    ppermute x4, waiting for transfers between devices, passed_along(): return lax.ppermute(block, axis, route)  5.62 us
    reduce_sum x2, other arithmetic, attend_block(): totals = jnp.sum(weights, axis=3)  5.58 us
    all_to_all x1, waiting for transfers between devices, body(): lax.all_to_all(key_rows, 'uly', split_axis=1, concat_axis=0, tiled=True)  4.81 us
    all_to_all x1, starting transfers between devices, body(): lax.all_to_all(key_rows, 'uly', split_axis=1, concat_axis=0, tiled=True)  4.4 us
    gather x2, local copies, waits for them, and re-layouts, attend_block(): value_buffer[slot_block]  3.92 us
  transfers between devices with their start and end apart: 7, of which 3 were waited for; matrix products, arithmetic and copies ran while one was open for 8% of the time, Pallas kernels for 0%

commit v1 on v0

v1 whole, which is shorter than its diff:
```python
import functools
import math

import jax
import jax.numpy as jnp
from jax import lax
from jax.experimental import pallas as pl
from jax.experimental.pallas import tpu as pltpu
from jax.sharding import PartitionSpec as P

HEAD_DIM = 128
TILE = 384
KEEP = 6
MESH = pl.DeviceIdType.MESH
EXP_SCALE = HEAD_DIM ** (-0.5) * math.log2(math.e)


def partner(me, step, n):
    found, bit = me, 1
    while bit < n:
        found = found + ((step // bit) % 2) * bit * (1 - 2 * ((me // bit) % 2))
        bit *= 2
    return found


def kernel(n_uly, n_blk, kept, q_in, k_in, v_in, out, q_buf, k_buf, v_buf, o_buf,
           split_send, split_recv, own_sem, halo_send, halo_recv, out_send, out_recv, out_sem):
    me = lax.axis_index("uly")
    slab = lax.axis_index("blk")
    has_prev, has_next = slab > 0, slab < n_blk - 1
    sides = ((has_prev, slab - 1, 2), (has_next, slab + 1, 0))

    def head_of(ref, head):
        return ref.at[:, pl.ds(pl.multiple_of(head * HEAD_DIM, HEAD_DIM), HEAD_DIM)]

    arrays = ((k_in, k_buf, n_uly), (v_in, v_buf, n_uly), (q_in, q_buf, 0))

    def split(kind, step):
        source, target, base = arrays[kind]
        peer = partner(me, step, n_uly)
        return pltpu.make_async_remote_copy(
            src_ref=head_of(source, peer), dst_ref=target.at[base + me],
            send_sem=split_send.at[kind, step], recv_sem=split_recv.at[kind, step],
            device_id=(peer, slab), device_id_type=MESH)

    def own(kind):
        source, target, base = arrays[kind]
        return pltpu.make_async_copy(head_of(source, me), target.at[base + me], own_sem.at[kind])

    def halo(kind, step, side):
        _, other, slot = sides[side]
        source, target, base = arrays[kind]
        position = partner(me, step, n_uly)
        held = head_of(source, me) if isinstance(step, int) and step == 0 else target.at[base + position]
        return pltpu.make_async_remote_copy(
            src_ref=held, dst_ref=target.at[slot * n_uly + position],
            send_sem=halo_send.at[kind, side, step], recv_sem=halo_recv.at[kind, side, step],
            device_id=(me, other), device_id_type=MESH)

    def give(step):
        peer = partner(me, step, n_uly)
        return pltpu.make_async_remote_copy(
            src_ref=o_buf.at[step], dst_ref=head_of(out, me),
            send_sem=out_send.at[step], recv_sem=out_recv.at[step],
            device_id=(peer, slab), device_id_type=MESH)

    barrier = pltpu.get_barrier_semaphore()
    for step in range(1, n_uly):
        pl.semaphore_signal(barrier, inc=1, device_id=(partner(me, step, n_uly), slab), device_id_type=MESH)
    for there, other, _ in sides:
        @pl.when(there)
        def _():
            pl.semaphore_signal(barrier, inc=1, device_id=(me, other), device_id_type=MESH)
    for kind in range(3):
        own(kind).start()
    pl.semaphore_wait(barrier, n_uly - 1 + has_prev.astype(jnp.int32) + has_next.astype(jnp.int32))

    order = [n_uly - 1] + list(range(1, n_uly - 1))
    for kind in range(2):
        for step in order:
            split(kind, step).start()
    for side, (there, _, _) in enumerate(sides):
        @pl.when(there)
        def _():
            for kind in range(2):
                halo(kind, 0, side).start()
    for step in order:
        split(2, step).start()
    for kind in range(2):
        for step in order:
            split(kind, step).wait_recv()
            for side, (there, _, _) in enumerate(sides):
                @pl.when(there)
                def _():
                    halo(kind, step, side).start()
    for kind in range(3):
        own(kind).wait()
    for side, (there, _, _) in enumerate(sides):
        @pl.when(there)
        def _():
            for kind in range(2):
                for step in range(n_uly):
                    halo(kind, step, 1 - side).wait_recv()

    def attend(turn, carry):
        step = lax.rem(turn + 1, n_uly)
        position = partner(me, step, n_uly)

        @pl.when(step > 0)
        def _():
            split(2, step).wait_recv()

        query = q_buf[position]
        slots, lifts = [], []
        for entry in range(KEEP):
            listed = kept[position * n_blk + slab, entry]
            live = listed >= 0
            slot = (listed % n_blk - slab + 1) * n_uly + listed // n_blk
            slots.append(jnp.clip(jnp.where(live, slot, n_uly + position), 0, 3 * n_uly - 1))
            lifts.append(jnp.where(live, 0.0, jnp.inf).astype(jnp.float32))
        scores, top = [], None
        for slot in slots:
            part = lax.dot_general(query, k_buf[slot], (((1,), (1,)), ((), ())),
                                   preferred_element_type=jnp.float32)
            scores.append(part)
            top = part if top is None else jnp.maximum(top, part)
        row_max = jnp.max(top, axis=1, keepdims=True) * EXP_SCALE
        mixed, sums = None, None
        for slot, lift, part in zip(slots, lifts, scores):
            weights = jnp.exp2(part * EXP_SCALE - (row_max + lift))
            sums = weights if sums is None else sums + weights
            term = jnp.dot(weights.astype(jnp.bfloat16), v_buf[slot], preferred_element_type=jnp.float32)
            mixed = term if mixed is None else mixed + term
        totals = jnp.sum(sums, axis=1, keepdims=True)
        o_buf[step] = (mixed / totals).astype(jnp.bfloat16)

        @pl.when(step > 0)
        def _():
            give(step).start()

        return carry

    lax.fori_loop(0, n_uly, attend, 0)
    last = pltpu.make_async_copy(o_buf.at[0], head_of(out, me), out_sem)
    last.start()
    for kind in range(3):
        for step in order:
            split(kind, step).wait_send()
    for side, (there, _, _) in enumerate(sides):
        @pl.when(there)
        def _():
            for kind in range(2):
                for step in range(n_uly):
                    halo(kind, step, side).wait_send()
    for step in order:
        peer = partner(me, step, n_uly)
        give(step).wait_send()
        pltpu.make_async_remote_copy(
            src_ref=o_buf.at[step], dst_ref=head_of(out, peer),
            send_sem=out_send.at[step], recv_sem=out_recv.at[step],
            device_id=(peer, slab), device_id_type=MESH).wait_recv()
    last.wait()


def body(n_uly, n_blk, query_rows, key_rows, value_rows, kept_tiles):
    flops = 4 * n_uly * KEEP * TILE * TILE * HEAD_DIM
    dma = pltpu.SemaphoreType.DMA
    tile = (TILE, HEAD_DIM)
    return pl.pallas_call(
        functools.partial(kernel, n_uly, n_blk),
        out_shape=jax.ShapeDtypeStruct(query_rows.shape, query_rows.dtype),
        in_specs=[pl.BlockSpec(memory_space=pltpu.SMEM)] + [pl.BlockSpec(memory_space=pl.ANY)] * 3,
        out_specs=pl.BlockSpec(memory_space=pltpu.VMEM),
        scratch_shapes=[
            pltpu.VMEM((n_uly, *tile), jnp.bfloat16),
            pltpu.VMEM((3 * n_uly, *tile), jnp.bfloat16),
            pltpu.VMEM((3 * n_uly, *tile), jnp.bfloat16),
            pltpu.VMEM((n_uly, *tile), jnp.bfloat16),
            dma((3, n_uly)), dma((3, n_uly)), dma((3,)),
            dma((2, 2, n_uly)), dma((2, 2, n_uly)),
            dma((n_uly,)), dma((n_uly,)), dma,
        ],
        compiler_params=pltpu.CompilerParams(
            collective_id=0, has_side_effects=True, vmem_limit_bytes=48 * 2**20),
        cost_estimate=pl.CostEstimate(
            flops=flops, bytes_accessed=8 * TILE * n_uly * HEAD_DIM,
            transcendentals=n_uly * KEEP * TILE * TILE),
    )(kept_tiles, query_rows, key_rows, value_rows)


def solution(mesh):
    rows = P(("uly", "blk"), None)
    return jax.shard_map(
        functools.partial(body, mesh.shape["uly"], mesh.shape["blk"]),
        mesh=mesh, in_specs=(rows, rows, rows, P()), out_specs=rows, check_vma=False)
```

time: 82.2 us -> 34.6 us (0.42)
  Pallas kernels: 0 us -> 29.6 us
  starting transfers between devices: 24.4 us -> 0 us
  matrix products: 12.8 us -> 0 us
  local copies, waits for them, and re-layouts: 16.4 us -> 4.5 us
  waiting for transfers between devices: 10.4 us -> 0 us
  blocking collectives: 8.99 us -> 0 us
  other arithmetic: 7.78 us -> 0 us
    pallas_call x0 -> x1, Pallas kernels: none -> 29.6 us  [body(): pl.pallas_call(functools.partial(kernel, n_uly, n_blk), out_shape=jax.Sha...]
    dot_general x4 -> x0, matrix products: 12.8 us -> none  [the longest x2 10.4 us: attend_block(): jnp.einsum('ghij,gjhd->gihd', weights_low, value_gather, preferred_elemen...]
    ppermute x4 -> x0, starting transfers between devices: 12.7 us -> none  [passed_along(): return lax.ppermute(block, axis, route)]
    all_to_all x3 -> x0, starting transfers between devices: 11.7 us -> none  [the longest x1 4.4 us: body(): lax.all_to_all(key_rows, 'uly', split_axis=1, concat_axis=0, tiled=True)]
    all_to_all x1 -> x0, blocking collectives: 8.99 us -> none  [body(): lax.all_to_all(attended, 'uly', split_axis=0, concat_axis=1, tiled=True)]
    gather x5 -> x0, local copies, waits for them, and re-layouts: 6.02 us -> none  [the longest x2 3.92 us: attend_block(): value_buffer[slot_block]]
    ppermute x4 -> x0, waiting for transfers between devices: 5.62 us -> none  [passed_along(): return lax.ppermute(block, axis, route)]
    reduce_sum x2 -> x0, other arithmetic: 5.58 us -> none  [attend_block(): totals = jnp.sum(weights, axis=3)]
  transfers between devices with their start and end apart: 7 -> 0, of which waited for: 3 -> 0; matrix products, arithmetic and copies ran while one was open for 8% -> 0% of each run, Pallas kernels for 0% -> 0%
where the time goes in v1:
time: 34.6 us; the launch traced here: 34.1 us
  Pallas kernels  29.6 us (86%)
  local copies, waits for them, and re-layouts  4.5 us (13%)
    pallas_call x1, Pallas kernels, body(): pl.pallas_call(functools.partial(kernel, n_uly, n_blk), out_shape=jax.Sha...  29.6 us
    unnamed x8, local copies, waits for them, and re-layouts  4.5 us

profile of v1, /device:TPU:1, one launch (start us, length us, event | category | flops | bytes accessed | tf_op | source)
XLA Modules:
  0.0 34.1 jit_solution(4607535865851603790)
XLA Ops:
  0.0 0.8 %copy.5.kept = s32[32,6]{1,0:T(8,128)S(1)} copy(s32[32,6]{0,1:T(8,128)} %param.7) | data formatting | bytes 1536 | tf_op args[3]
  0.8 0.0 copy-start
  0.8 1.0 %copy-done = bf16[384,512]{1,0:T(8,128)(2,1)S(1)} copy-done((bf16[384,512]{1,0:T(8,128)(2,1)S(1)}, bf16[384,512]{1,0:T(8,128)(2,1)}, u32[]{:S(2)}) %copy-start) | copy-done | bytes 393240
  1.8 0.0 copy-start.1
  1.8 1.0 %copy-done.1 = bf16[384,512]{1,0:T(8,128)(2,1)S(1)} copy-done((bf16[384,512]{1,0:T(8,128)(2,1)S(1)}, bf16[384,512]{1,0:T(8,128)(2,1)}, u32[]{:S(2)}) %copy-start.1) | copy-done | bytes 393240
  2.8 0.0 copy-start.2
  2.8 1.0 %copy-done.2 = bf16[384,512]{1,0:T(8,128)(2,1)S(1)} copy-done((bf16[384,512]{1,0:T(8,128)(2,1)S(1)}, bf16[384,512]{1,0:T(8,128)(2,1)}, u32[]{:S(2)}) %copy-start.2) | copy-done | bytes 393240
  3.8 29.6 %shard_map.46 = bf16[384,512]{1,0:T(8,128)(2,1)S(1)} custom-call(s32[32,6]{1,0:T(8,128)S(1)} %copy.5.kept, bf16[384,512]{1,0:T(8,128)(2,1)S(1)} %copy-done, bf16[384,512]{1,0:T(8,128)(2,1)S(1)} %copy-done.1, bf16[384,512]{1,0:T(8,128)(2,1)S(1)} %copy-done.2), custom_call_target="tpu_custom_call" | custom-call | flops 1811939328 | bytes 1572864 | tf_op jit(solution)/shard_map/pallas_call | solution.py:169
  33.4 0.7 %copy.7 = bf16[384,512]{1,0:T(8,128)(2,1)} copy(bf16[384,512]{1,0:T(8,128)(2,1)S(1)} %shard_map.46) | data formatting | bytes 786432
Async XLA Ops:
  0.8 1.0 %copy-start = (bf16[384,512]{1,0:T(8,128)(2,1)S(1)}, bf16[384,512]{1,0:T(8,128)(2,1)}, u32[]{:S(2)}) copy-start(bf16[384,512]{1,0:T(8,128)(2,1)} %q_in.1) | copy-start | bytes 1179652
  1.8 1.0 %copy-start.1 = (bf16[384,512]{1,0:T(8,128)(2,1)S(1)}, bf16[384,512]{1,0:T(8,128)(2,1)}, u32[]{:S(2)}) copy-start(bf16[384,512]{1,0:T(8,128)(2,1)} %k_in.1) | copy-start | bytes 1179652
  2.8 1.0 %copy-start.2 = (bf16[384,512]{1,0:T(8,128)(2,1)S(1)}, bf16[384,512]{1,0:T(8,128)(2,1)}, u32[]{:S(2)}) copy-start(bf16[384,512]{1,0:T(8,128)(2,1)} %v_in.1) | copy-start | bytes 1179652

commit v2 on v1

--- a/solution.py
+++ b/solution.py
@@ -23,8 +23,8 @@
     return found
 
 
-def kernel(n_uly, n_blk, kept, q_in, k_in, v_in, out, q_buf, k_buf, v_buf, o_buf,
-           split_send, split_recv, own_sem, halo_send, halo_recv, out_send, out_recv, out_sem):
+def kernel(n_uly, n_blk, kept_in, q_in, k_in, v_in, out, q_buf, k_buf, v_buf, o_buf,
+           split_send, split_recv, own_sem, halo_send, halo_recv, out_send, out_recv, out_sem, kept, kept_sem):
     me = lax.axis_index("uly")
     slab = lax.axis_index("blk")
     has_prev, has_next = slab > 0, slab < n_blk - 1
@@ -73,6 +73,8 @@
             pl.semaphore_signal(barrier, inc=1, device_id=(me, other), device_id_type=MESH)
     for kind in range(3):
         own(kind).start()
+    lists = pltpu.make_async_copy(kept_in, kept, kept_sem)
+    lists.start()
     pl.semaphore_wait(barrier, n_uly - 1 + has_prev.astype(jnp.int32) + has_next.astype(jnp.int32))
 
     order = [n_uly - 1] + list(range(1, n_uly - 1))
@@ -95,6 +97,7 @@
                     halo(kind, step, side).start()
     for kind in range(3):
         own(kind).wait()
+    lists.wait()
     for side, (there, _, _) in enumerate(sides):
         @pl.when(there)
         def _():
@@ -103,7 +106,7 @@
                     halo(kind, step, 1 - side).wait_recv()
 
     def attend(turn, carry):
-        step = lax.rem(turn + 1, n_uly)
+        step = jnp.where(turn == 0, n_uly - 1, jnp.where(turn == n_uly - 1, 0, turn))
         position = partner(me, step, n_uly)
 
         @pl.when(step > 0)
@@ -169,7 +172,7 @@
     return pl.pallas_call(
         functools.partial(kernel, n_uly, n_blk),
         out_shape=jax.ShapeDtypeStruct(query_rows.shape, query_rows.dtype),
-        in_specs=[pl.BlockSpec(memory_space=pltpu.SMEM)] + [pl.BlockSpec(memory_space=pl.ANY)] * 3,
+        in_specs=[pl.BlockSpec(memory_space=pltpu.HBM)] * 4,
         out_specs=pl.BlockSpec(memory_space=pltpu.VMEM),
         scratch_shapes=[
             pltpu.VMEM((n_uly, *tile), jnp.bfloat16),
@@ -179,6 +182,7 @@
             dma((3, n_uly)), dma((3, n_uly)), dma((3,)),
             dma((2, 2, n_uly)), dma((2, 2, n_uly)),
             dma((n_uly,)), dma((n_uly,)), dma,
+            pltpu.SMEM(kept_tiles.shape, jnp.int32), dma,
         ],
         compiler_params=pltpu.CompilerParams(
             collective_id=0, has_side_effects=True, vmem_limit_bytes=48 * 2**20),

time: 34.6 us -> 32 us (0.925)
  Pallas kernels: 29.6 us -> 27.2 us
    pallas_call x1, Pallas kernels: 29.6 us -> 27.2 us  [body(): pl.pallas_call(functools.partial(kernel, n_uly, n_blk), out_shape=jax.Sha...]
where the time goes in v2:
time: 32 us; the launch traced here: 31.8 us
  Pallas kernels  27.2 us (85%)
  local copies, waits for them, and re-layouts  4.5 us (14%)
    pallas_call x1, Pallas kernels, body(): pl.pallas_call(functools.partial(kernel, n_uly, n_blk), out_shape=jax.Sha...  27.2 us
    unnamed x8, local copies, waits for them, and re-layouts  4.5 us

profile of v2, /device:TPU:1, one launch (start us, length us, event | category | flops | bytes accessed | tf_op | source)
XLA Modules:
  0.0 31.8 jit_solution(10510768820113727786)
XLA Ops:
  0.0 0.8 %copy.5.kept_in = s32[32,6]{1,0:T(8,128)S(1)} copy(s32[32,6]{0,1:T(8,128)} %param.7) | data formatting | bytes 1536 | tf_op args[3]
  0.8 0.0 copy-start
  0.8 1.0 %copy-done = bf16[384,512]{1,0:T(8,128)(2,1)S(1)} copy-done((bf16[384,512]{1,0:T(8,128)(2,1)S(1)}, bf16[384,512]{1,0:T(8,128)(2,1)}, u32[]{:S(2)}) %copy-start) | copy-done | bytes 393240
  1.8 0.0 copy-start.1
  1.8 1.0 %copy-done.1 = bf16[384,512]{1,0:T(8,128)(2,1)S(1)} copy-done((bf16[384,512]{1,0:T(8,128)(2,1)S(1)}, bf16[384,512]{1,0:T(8,128)(2,1)}, u32[]{:S(2)}) %copy-start.1) | copy-done | bytes 393240
  2.8 0.0 copy-start.2
  2.8 1.0 %copy-done.2 = bf16[384,512]{1,0:T(8,128)(2,1)S(1)} copy-done((bf16[384,512]{1,0:T(8,128)(2,1)S(1)}, bf16[384,512]{1,0:T(8,128)(2,1)}, u32[]{:S(2)}) %copy-start.2) | copy-done | bytes 393240
  3.8 27.2 %shard_map.46 = bf16[384,512]{1,0:T(8,128)(2,1)S(1)} custom-call(s32[32,6]{1,0:T(8,128)S(1)} %copy.5.kept_in, bf16[384,512]{1,0:T(8,128)(2,1)S(1)} %copy-done, bf16[384,512]{1,0:T(8,128)(2,1)S(1)} %copy-done.1, bf16[384,512]{1,0:T(8,128)(2,1)S(1)} %copy-done.2), custom_call_target="tpu_custom_call" | custom-call | flops 1811939328 | bytes 1572864 | tf_op jit(solution)/shard_map/pallas_call | solution.py:172
  31.0 0.7 %copy.7 = bf16[384,512]{1,0:T(8,128)(2,1)} copy(bf16[384,512]{1,0:T(8,128)(2,1)S(1)} %shard_map.46) | data formatting | bytes 786432
Async XLA Ops:
  0.8 1.0 %copy-start = (bf16[384,512]{1,0:T(8,128)(2,1)S(1)}, bf16[384,512]{1,0:T(8,128)(2,1)}, u32[]{:S(2)}) copy-start(bf16[384,512]{1,0:T(8,128)(2,1)} %q_in.1) | copy-start | bytes 1179652
  1.8 1.0 %copy-start.1 = (bf16[384,512]{1,0:T(8,128)(2,1)S(1)}, bf16[384,512]{1,0:T(8,128)(2,1)}, u32[]{:S(2)}) copy-start(bf16[384,512]{1,0:T(8,128)(2,1)} %k_in.1) | copy-start | bytes 1179652
  2.8 1.0 %copy-start.2 = (bf16[384,512]{1,0:T(8,128)(2,1)S(1)}, bf16[384,512]{1,0:T(8,128)(2,1)}, u32[]{:S(2)}) copy-start(bf16[384,512]{1,0:T(8,128)(2,1)} %v_in.1) | copy-start | bytes 1179652
